TPU v7x, 256 devices: a whole 4x4x8 slice. The times are simulated.
256 devices in a mesh: dp: 32 (over x, z), seq: 8 (over y, core).
Axes of the slice: x: 4, y: 4, z: 8, core: 2. Of those that a mesh axis runs over, the one named last changes fastest.
Arguments:
- pixels: bfloat16 [32768, 1176], P(('dp', 'seq')), may hold values from -6 to 6
- patch_weight: bfloat16 [1176, 1280], replicated, may hold values from -0.1875 to 0.1875
- ln_gain: float32 [1280], replicated, may hold values from 0.1 to 1.9
- ln_bias: float32 [1280], replicated, may hold values from -1.5 to 1.5
- qkv_weight: bfloat16 [1280, 3840], P('dp'), may hold values from -4 to 4
- qkv_bias: float32 [3840], replicated, may hold values from -2.5 to 2.5
- out_weight: bfloat16 [1280, 1280], P('dp'), may hold values from -0.15625 to 0.15625
- out_bias: float32 [1280], replicated, may hold values from -1.5 to 1.5
- offsets: int32 [32, 3], P('dp'), may hold values from 0 to 854, as said below
- widths: int32 [32, 3], P('dp'), may hold values from 16 to 64
Outputs:
- encoded: bfloat16 [32768, 1280], P(('dp', 'seq'))
Inputs may be any that keep to these rules, and one draw needn't show every extreme that they name: In every group the first offset is 0 and offsets rise; every image holds 170 or more tokens and the last image ends at position 1024; in some group the last image holds exactly 170 tokens.
All inputs are finite; a program needn't handle non-finite values.
Results may differ from a plain program's by a relative error of at most 0.012.
Values may be sent and summed in bfloat16 or wider, within the bound.
No kernel may reach another device: no remote copies, remote signals or barrier semaphores. Data moves between devices by JAX's collectives and lax.ppermute only.
A program may use at most 64 MiB of HBM per device.

v0:
```python
import jax
import jax.numpy as jnp
from jax import lax
from jax.sharding import PartitionSpec as P

HEADS = 16
HDIM = 80


def image_lookup(positions, starts):
    return jnp.sum((positions[:, None] >= starts[None, :]).astype(jnp.int32), axis=1) - 1


def rotation_tables(positions, starts, image_widths, head_size):
    image_index = image_lookup(positions, starts)
    onehot = (image_index[:, None] == jnp.arange(starts.shape[0], dtype=jnp.int32)[None, :]).astype(
        jnp.int32
    )
    first_position = jnp.sum(onehot * starts[None, :], axis=1)
    across = jnp.sum(onehot * image_widths[None, :], axis=1)
    within = positions - first_position
    row_index = within // across
    column_index = within - row_index * across
    quarter = head_size // 4
    inverse = 1.0 / 10000.0 ** (jnp.arange(quarter, dtype=jnp.float32) * 2.0 / (head_size // 2))
    angles = jnp.concatenate(
        [
            row_index.astype(jnp.float32)[:, None] * inverse[None, :],
            column_index.astype(jnp.float32)[:, None] * inverse[None, :],
        ],
        axis=1,
    )
    angles = jnp.concatenate([angles, angles], axis=1)
    return (jnp.cos(angles), jnp.sin(angles), image_index)


def rotate_heads(values, cosine, sine_table, head_size):
    half_size = head_size // 2
    turned = jnp.concatenate([-values[..., half_size:], values[..., :half_size]], axis=-1)
    return values * cosine[:, None, :] + turned * sine_table[:, None, :]


def layer_norm(embedded, ln_gain, ln_bias):
    values = embedded.astype(jnp.float32)
    center = values - jnp.mean(values, axis=-1, keepdims=True)
    variance = jnp.mean(center * center, axis=-1, keepdims=True)
    return (center * lax.rsqrt(variance + 1e-06) * ln_gain + ln_bias).astype(jnp.bfloat16)


def block_length(count):
    length = min(count, 512)
    while count % length:
        length -= 1
    return length


def attend_block(state, queries3, key_block, value_block, query_image, key_image, score_scale):
    running_max, running_total, accum = state
    count = key_block.shape[0]
    scores = (
        jnp.einsum(
            "qhd,khd->hqk",
            queries3,
            key_block.reshape(count, HEADS, HDIM),
            preferred_element_type=jnp.float32,
        )
        * score_scale
    )
    allowed = (query_image[:, None] == key_image[None, :])[None]
    scores = jnp.where(allowed, scores, -1e30)
    new_max = jnp.maximum(running_max, jnp.max(scores, axis=-1))
    weights = jnp.where(allowed, jnp.exp(scores - new_max[..., None]), 0.0)
    factor = jnp.exp(running_max - new_max)
    running_total = running_total * factor + jnp.sum(weights, axis=-1)
    part_sum = jnp.einsum(
        "hqk,khd->qhd",
        weights.astype(jnp.bfloat16),
        value_block.reshape(count, HEADS, HDIM),
        preferred_element_type=jnp.float32,
    )
    accum = accum * factor.T[:, :, None] + part_sum
    return (new_max, running_total, accum)


def per_device(
    pixels,
    patch_weight,
    ln_gain,
    ln_bias,
    qkv_weight,
    qkv_bias,
    out_weight,
    out_bias,
    offsets,
    widths,
):
    local_pixels = lax.all_to_all(pixels, "dp", split_axis=0, concat_axis=0, tiled=True)
    tok_rows = local_pixels.shape[0]
    dmodel = patch_weight.shape[1]
    score_scale = HDIM ** (-0.5)
    embedded = jnp.dot(local_pixels, patch_weight, preferred_element_type=jnp.float32).astype(
        jnp.bfloat16
    )
    normed = layer_norm(embedded, ln_gain, ln_bias)
    columns = normed
    projected = (
        jnp.dot(
            columns,
            lax.all_gather(qkv_weight, "dp", axis=0, tiled=True),
            preferred_element_type=jnp.float32,
        )
        + qkv_bias
    )
    starts = offsets[0]
    image_widths = widths[0]
    positions = lax.axis_index("seq") * tok_rows + jnp.arange(tok_rows, dtype=jnp.int32)
    cosine, sine_table, query_image = rotation_tables(positions, starts, image_widths, HDIM)
    queries = (
        rotate_heads(projected[:, :dmodel].reshape(tok_rows, HEADS, HDIM), cosine, sine_table, HDIM)
        .reshape(tok_rows, dmodel)
        .astype(jnp.bfloat16)
    )
    key_rows = (
        rotate_heads(
            projected[:, dmodel : 2 * dmodel].reshape(tok_rows, HEADS, HDIM),
            cosine,
            sine_table,
            HDIM,
        )
        .reshape(tok_rows, dmodel)
        .astype(jnp.bfloat16)
    )
    values = projected[:, 2 * dmodel :].astype(jnp.bfloat16)
    queries3 = queries.reshape(tok_rows, HEADS, HDIM)
    initial = (
        jnp.full((HEADS, tok_rows), -1e30, jnp.float32),
        jnp.zeros((HEADS, tok_rows), jnp.float32),
        jnp.zeros((tok_rows, HEADS, HDIM), jnp.float32),
    )
    piece_keys = lax.all_gather(key_rows, "seq", axis=0, tiled=True)
    piece_values = lax.all_gather(values, "seq", axis=0, tiled=True)
    count = piece_keys.shape[0]
    length = block_length(count)

    def one_block(block_index, inner):
        first_row = block_index * length
        key_block = lax.dynamic_slice_in_dim(piece_keys, first_row, length, 0)
        value_block = lax.dynamic_slice_in_dim(piece_values, first_row, length, 0)
        key_image = image_lookup(first_row + jnp.arange(length, dtype=jnp.int32), starts)
        return attend_block(
            inner, queries3, key_block, value_block, query_image, key_image, score_scale
        )

    final_state = lax.fori_loop(0, count // length, one_block, initial)
    attended = (
        (final_state[2] / final_state[1].T[:, :, None])
        .reshape(tok_rows, dmodel)
        .astype(jnp.bfloat16)
    )
    columns = attended
    mixed = jnp.dot(
        columns,
        lax.all_gather(out_weight, "dp", axis=0, tiled=True),
        preferred_element_type=jnp.float32,
    )
    return (embedded.astype(jnp.float32) + mixed + out_bias).astype(jnp.bfloat16)


def solution(mesh):
    in_specs = (
        P(("dp", "seq"), None),
        P(),
        P(),
        P(),
        P("dp", None),
        P(),
        P("dp", None),
        P(),
        P("dp", None),
        P("dp", None),
    )
    out_specs = P(("dp", "seq"), None)
    return jax.shard_map(
        per_device, mesh=mesh, in_specs=in_specs, out_specs=out_specs, check_vma=False
    )
```

profile of v0, /device:TPU:8, one launch (start us, length us, event | category | flops | bytes accessed | tf_op | source)
XLA Modules:
  0.0 290.6 jit_solution(15201041775588603741)
XLA Ops:
  6.5 0.0 copy-start
  6.5 0.0 all-gather.5.cloned.1.call-start
  6.5 0.7 all-gather.5.cloned.1.call-update
  7.3 1.3 copy.27
  8.6 0.8 all_to_all.8
  9.4 11.4 %all-to-all-start = ((bf16[32,4,1176]{2,1,0:T(4,128)(2,1)}), bf16[32,4,1176]{2,1,0:T(4,128)(2,1)}, u32[]{:S(2)}, u32[]{:S(2)}) async-start(bf16[32,4,1176]{2,1,0:T(4,128)(2,1)} %all_to_all.8), calls=%async_computation | async-start | bytes 655360 | tf_op jit(solution)/shard_map/all_to_all | solution.py:97
  20.8 0.0 all-gather.7.cloned.1.call-start
  20.9 0.7 convert_reduce_fusion.1
  21.6 0.8 select_reduce_fusion.1
  22.4 0.1 fusion.26
  22.6 0.1 broadcast_multiply_fusion.1
  22.6 0.2 fusion.25
  22.8 0.9 mul.198
  23.7 2.2 copy.28
  25.9 8.5 %all-to-all-done = bf16[32,4,1176]{2,1,0:T(4,128)(2,1)} async-done(((bf16[32,4,1176]{2,1,0:T(4,128)(2,1)}), bf16[32,4,1176]{2,1,0:T(4,128)(2,1)}, u32[]{:S(2)}, u32[]{:S(2)}) %all-to-all-start) | async-done | bytes 301088 | tf_op jit(solution)/shard_map/all_to_all | solution.py:97
  34.4 1.1 all_to_all.10
  35.5 0.0 copy-done
  35.5 0.7 fusion.28
  36.2 0.0 copy-start.2
  36.2 0.8 copy-done.2
  37.1 0.2 multiply_reduce_fusion
  37.3 81.0 %all-gather.5.cloned.1.call-done = bf16[1280,3840]{1,0:T(8,128)(2,1)} async-done(((bf16[40,3840]{1,0:T(8,128)(2,1)}), bf16[1280,3840]{1,0:T(8,128)(2,1)}) %all-gather.5.cloned.1.call-update) | async-done | bytes 9830416 | tf_op jit(solution)/shard_map/all_gather | solution.py:109
  118.3 0.0 copy-done.4
  118.3 5.5 %convolution_add_fusion = f32[128,3840]{1,0:T(8,128)S(1)} fusion(bf16[1280,3840]{1,0:T(8,128)(2,1)} %all-gather.5.cloned.1.call-done, f32[3840]{0:T(1024)S(1)} %copy-done.7, f32[128,1280]{1,0:T(8,128)} %copy-done.2, f32[1280]{0:T(1024)S(1)} %copy-done.4, f32[1280]{0:T(1024)S(1)} %copy-done.5, f32[128]{0:T(128)S(1)} %add_rsqrt_fusion, ...), kind=kOutput, calls=%fused_computation.24 | convolution fusion | flops 1259601920 | bytes 12478464 | tf_op jit(solution)/shard_map/dot_general | solution.py:107
  123.8 1.3 copy-done.3
  125.1 1.1 fusion.27
  126.3 2.1 copy.29
  128.4 2.2 copy.32
  130.6 1.4 slice_negate_fusion
  131.9 1.2 maximum_multiply_fusion.1
  133.1 2.2 copy.30
  135.2 2.2 copy.33
  137.4 2.9 add_convert_fusion
  140.3 0.0 all-gather.7.cloned.1.call-update
  140.3 0.0 all-gather.9.cloned.1.call-start
  140.4 1.8 slice.41
  142.2 0.0 all-gather.9.cloned.1.call-update
  142.2 0.0 all-gather.11.cloned.1.call-start
  142.3 0.5 all-gather.11.cloned.1.call-update
  142.8 1.2 copy.34
  144.0 21.3 %all-gather.7.cloned.1.call-done = bf16[1024,1280]{1,0:T(8,128)(2,1)} async-done(((bf16[128,1280]{1,0:T(8,128)(2,1)}), bf16[1024,1280]{1,0:T(8,128)(2,1)}) %all-gather.7.cloned.1.call-update) | async-done | bytes 2621456 | tf_op jit(solution)/shard_map/all_gather | solution.py:140
  165.3 31.1 %all-gather.9.cloned.1.call-done = bf16[1024,1280]{1,0:T(8,128)(2,1)} async-done(((bf16[128,1280]{1,0:T(8,128)(2,1)}), bf16[1024,1280]{1,0:T(8,128)(2,1)}) %all-gather.9.cloned.1.call-update) | async-done | bytes 2621456 | tf_op jit(solution)/shard_map/all_gather | solution.py:141
  196.5 37.7 %while.20 = (s32[]{:T(128)}, f32[16,128]{1,0:T(8,128)S(1)}, f32[16,128]{1,0:T(8,128)S(1)}, f32[128,16,80]{0,2,1:T(8,128)}, s32[128]{0:T(128)S(1)}, /*index=5*/s3...) while((s32[]{:T(128)}, f32[16,128]{1,0:T(8,128)S(1)}, ...), condition=%wide.region_9.10_spmd.clone, body=%wide.region_5.9_spmd.clone.sunk | while | flops 349750272 | bytes 44511972 | solution.py:154
  196.5 3.5 %constant_dynamic-slice_fusion.3 = (bf16[512,1280]{1,0:T(8,128)(2,1)}, bf16[512,1280]{1,0:T(8,128)(2,1)}) fusion(bf16[1024,1280]{1,0:T(8,128)(2,1)} %get-tuple-element.432, s32[]{:T(128)S(6)} %select_n.85, bf16[1024,1280]{1,0:T(8,128)(2,1)} %get-tuple-element.430), kind=kLoop, calls=%fused_computation.19.clone.1 | loop fusion | bytes 5242884 | tf_op jit(solution)/shard_map/while/body/eval_jaxpr/dynamic_slice | solution.py:148
  199.9 2.4 copy.42
  202.4 0.1 convert_reduce_fusion.3
  202.5 0.1 broadcast_compare_fusion.2
  202.6 4.3 %fusion.50 = (f32[16,128]{1,0:T(8,128)S(1)}, f32[16,512,128]{2,1,0:T(8,128)}) fusion(pred[128,512]{0,1:T(8,128)(4,1)S(1)} %broadcast_compare_fusion.2, bf16[512,16,80]{0,2,1:T(8,128)(2,1)} %bitcast.64, bf16[128,16,80]{0,2,1:T(8,128)(2,1)S(1)} %get-tuple-element.431), kind=kOutput, calls=%fused_computation.2.clone.1 | convolution fusion | flops 170915840 | bytes 5906432 | tf_op jit(solution)/shard_map/while/body/eval_jaxpr/qhd,khd->hqk/dot_general | solution.py:61
  206.9 2.4 copy.43
  209.3 4.8 %fusion.54 = f32[128,16,80]{0,2,1:T(8,128)} fusion(bf16[512,16,80]{0,2,1:T(8,128)(2,1)} %bitcast.65, f32[16,512,128]{2,1,0:T(8,128)} %get-tuple-element.395, f32[16,128]{1,0:T(8,128)S(1)} %get-tuple-element.425, pred[128,512]{0,1:T(8,128)(4,1)S(1)} %broadcast_compare_fusion.2, f32[128,16,80]{0,2,1:T(8,128)} %get-tuple-element.414, ...), kind=kOutput, calls=%fused_computation.8.clone.1 | convolution fusion | flops 173506560 | bytes 6897665 | tf_op jit(solution)/shard_map/while/body/eval_jaxpr/hqk,khd->qhd/dot_general | solution.py:75
  214.2 0.0 copy-done.1
  214.2 1.0 fusion.52
  215.3 3.5 %constant_dynamic-slice_fusion.3 = (bf16[512,1280]{1,0:T(8,128)(2,1)}, bf16[512,1280]{1,0:T(8,128)(2,1)}) fusion(bf16[1024,1280]{1,0:T(8,128)(2,1)} %get-tuple-element.432, s32[]{:T(128)S(6)} %select_n.85, bf16[1024,1280]{1,0:T(8,128)(2,1)} %get-tuple-element.430), kind=kLoop, calls=%fused_computation.19.clone.1 | loop fusion | bytes 5242884 | tf_op jit(solution)/shard_map/while/body/eval_jaxpr/dynamic_slice | solution.py:148
  218.7 2.4 copy.42
  221.2 0.1 convert_reduce_fusion.3
  221.3 0.1 broadcast_compare_fusion.2
  221.4 4.3 %fusion.50 = (f32[16,128]{1,0:T(8,128)S(1)}, f32[16,512,128]{2,1,0:T(8,128)}) fusion(pred[128,512]{0,1:T(8,128)(4,1)S(1)} %broadcast_compare_fusion.2, bf16[512,16,80]{0,2,1:T(8,128)(2,1)} %bitcast.64, bf16[128,16,80]{0,2,1:T(8,128)(2,1)S(1)} %get-tuple-element.431), kind=kOutput, calls=%fused_computation.2.clone.1 | convolution fusion | flops 170915840 | bytes 5906432 | tf_op jit(solution)/shard_map/while/body/eval_jaxpr/qhd,khd->hqk/dot_general | solution.py:61
  225.7 2.4 copy.43
  228.1 5.0 %fusion.54 = f32[128,16,80]{0,2,1:T(8,128)} fusion(bf16[512,16,80]{0,2,1:T(8,128)(2,1)} %bitcast.65, f32[16,512,128]{2,1,0:T(8,128)} %get-tuple-element.395, f32[16,128]{1,0:T(8,128)S(1)} %get-tuple-element.425, pred[128,512]{0,1:T(8,128)(4,1)S(1)} %broadcast_compare_fusion.2, f32[128,16,80]{0,2,1:T(8,128)} %get-tuple-element.414, ...), kind=kOutput, calls=%fused_computation.8.clone.1 | convolution fusion | flops 173506560 | bytes 6897665 | tf_op jit(solution)/shard_map/while/body/eval_jaxpr/hqk,khd->qhd/dot_general | solution.py:75
  233.1 0.0 copy-done.1
  233.1 1.0 fusion.52
  234.2 1.1 divide_convert_fusion
  235.3 45.3 %all-gather.11.cloned.1.call-done = bf16[1280,1280]{1,0:T(8,128)(2,1)} async-done(((bf16[40,1280]{1,0:T(8,128)(2,1)}), bf16[1280,1280]{1,0:T(8,128)(2,1)}) %all-gather.11.cloned.1.call-update) | async-done | bytes 3276816 | tf_op jit(solution)/shard_map/all_gather | solution.py:163
  280.7 3.4 %fusion.18 = bf16[128,1280]{1,0:T(8,128)(2,1)} fusion(f32[128,1280]{1,0:T(8,128)} %copy-done.2, bf16[128,1280]{0,1:T(8,128)(2,1)S(1)} %bitcast.72, bf16[1280,1280]{1,0:T(8,128)(2,1)} %all-gather.11.cloned.1.call-done, f32[1280]{0:T(1024)S(1)} %copy-done.8), kind=kOutput, calls=%fused_computation.27 | convolution fusion | flops 419921920 | bytes 4592640 | tf_op jit(solution)/shard_map/dot_general | solution.py:161
  (31 shorter events, 0.1 us)
Async XLA Ops:
  6.5 29.0 %copy-start = (bf16[1176,1280]{1,0:T(8,128)(2,1)S(1)}, bf16[1176,1280]{1,0:T(8,128)(2,1)}, u32[]{:S(2)}) copy-start(bf16[1176,1280]{1,0:T(8,128)(2,1)} %param.13) | copy-start | bytes 9031684
  6.5 111.7 %all-gather.5.cloned.1.call-start = ((), (), s32[]{:S(2)}) async-start(), calls=%async_computation.1 | async-start | bytes 10137600 | tf_op jit(solution)/shard_map/all_gather | solution.py:109
  9.4 25.0 %all-to-all-start = ((bf16[32,4,1176]{2,1,0:T(4,128)(2,1)}), bf16[32,4,1176]{2,1,0:T(4,128)(2,1)}, u32[]{:S(2)}, u32[]{:S(2)}) async-start(bf16[32,4,1176]{2,1,0:T(4,128)(2,1)} %all_to_all.8), calls=%async_computation | async-start | bytes 655360 | tf_op jit(solution)/shard_map/all_to_all | solution.py:97
  20.8 144.5 %all-gather.7.cloned.1.call-start = ((), (), s32[]{:S(2)}) async-start(), calls=%async_computation.2 | async-start | bytes 2949120 | tf_op jit(solution)/shard_map/all_gather | solution.py:140
  23.7 94.6 %copy-start.4 = (f32[1280]{0:T(1024)S(1)}, f32[1280]{0:T(1024)}, u32[]{:S(2)}) copy-start(f32[1280]{0:T(1024)} %param.15) | copy-start | bytes 15364
  23.7 94.6 %copy-start.5 = (f32[1280]{0:T(1024)S(1)}, f32[1280]{0:T(1024)}, u32[]{:S(2)}) copy-start(f32[1280]{0:T(1024)} %param.14) | copy-start | bytes 15364
  23.7 94.6 %copy-start.7 = (f32[3840]{0:T(1024)S(1)}, f32[3840]{0:T(1024)}, u32[]{:S(2)}) copy-start(f32[3840]{0:T(1024)} %param.17) | copy-start | bytes 46084
  36.2 0.9 copy-start.2
  123.8 1.3 copy-start.3
  137.4 59.1 %copy-start.6 = (s32[1,3]{1,0:T(1,128)S(1)}, s32[1,3]{1,0:T(1,128)}, u32[]{:S(2)}) copy-start(s32[1,3]{1,0:T(1,128)} %param.20) | copy-start | bytes 40
  140.3 56.1 %all-gather.9.cloned.1.call-start = ((), (), s32[]{:S(2)}) async-start(), calls=%async_computation.3 | async-start | bytes 2949120 | tf_op jit(solution)/shard_map/all_gather | solution.py:141
  142.2 138.4 %all-gather.11.cloned.1.call-start = ((), (), s32[]{:S(2)}) async-start(), calls=%async_computation.4 | async-start | bytes 3379200 | tf_op jit(solution)/shard_map/all_gather | solution.py:163
  196.5 84.2 %copy-start.8 = (f32[1280]{0:T(1024)S(1)}, f32[1280]{0:T(1024)}, u32[]{:S(2)}) copy-start(f32[1280]{0:T(1024)} %param.19) | copy-start | bytes 15364
  209.3 4.9 %copy-start.1 = (f32[16,512,128]{2,1,0:T(8,128)S(1)}, f32[16,512,128]{2,1,0:T(8,128)}, u32[]{:S(2)}) copy-start(f32[16,512,128]{2,1,0:T(8,128)} %get-tuple-element.395) | copy-start | bytes 12582916 | tf_op jit(solution)/shard_map/while
  228.1 5.0 %copy-start.1 = (f32[16,512,128]{2,1,0:T(8,128)S(1)}, f32[16,512,128]{2,1,0:T(8,128)}, u32[]{:S(2)}) copy-start(f32[16,512,128]{2,1,0:T(8,128)} %get-tuple-element.395) | copy-start | bytes 12582916 | tf_op jit(solution)/shard_map/while
Sparse Core Ops, SparseCore 0:
  10.0 108.2 all-gather.4
  140.4 24.8 all-gather.6
  167.2 29.2 all-gather.8
  198.9 81.7 all-gather.10
where the time goes:
time: 291 us
  waiting for transfers between devices  188 us (65%)
  local copies, waits for them, and re-layouts  38 us (13%)
  matrix products  28.1 us (10%)
  between operations  13.3 us (5%)
  starting transfers between devices  11.6 us (4%)
  other arithmetic  11.2 us (4%)
    all_gather x1, waiting for transfers between devices, per_device(): lax.all_gather(qkv_weight, 'dp', axis=0, tiled=True)  81 us
    all_gather x1, waiting for transfers between devices, per_device(): lax.all_gather(out_weight, 'dp', axis=0, tiled=True)  45.3 us
    all_gather x1, waiting for transfers between devices, per_device(): piece_values = lax.all_gather(values, 'seq', axis=0, tiled=True)  31.1 us
    all_gather x1, waiting for transfers between devices, per_device(): piece_keys = lax.all_gather(key_rows, 'seq', axis=0, tiled=True)  21.3 us
    dynamic_slice x4, local copies, waits for them, and re-layouts, one_block(): value_block = lax.dynamic_slice_in_dim(piece_values, first_row, length, 0)  11.8 us
    all_to_all x1, starting transfers between devices, per_device(): lax.all_to_all(pixels, 'dp', split_axis=0, concat_axis=0, tiled=True)  11.4 us
    dot_general x2, matrix products, attend_block(): jnp.einsum('hqk,khd->qhd', weights.astype(jnp.bfloat16), value_block.resh...  9.84 us
    dot_general x2, matrix products, attend_block(): jnp.einsum('qhd,khd->hqk', queries3, key_block.reshape(count, HEADS, HDIM...  8.54 us
  transfers between devices with their start and end apart: 5, of which 5 were waited for; matrix products, arithmetic and copies ran while one was open for 17% of the time, Pallas kernels for 0%

commit v1 on v0

--- a/solution.py
+++ b/solution.py
@@ -137,7 +137,16 @@
         jnp.zeros((HEADS, tok_rows), jnp.float32),
         jnp.zeros((tok_rows, HEADS, HDIM), jnp.float32),
     )
-    piece_keys = lax.all_gather(key_rows, "seq", axis=0, tiled=True)
+    value = key_rows
+    ways, here, step = (lax.axis_size("seq"), lax.axis_index("seq"), value.shape[0])
+    shape = [n * ways if d == 0 else n for d, n in enumerate(value.shape)]
+    full = lax.dynamic_update_slice_in_dim(
+        jnp.zeros(shape, value.dtype), value, here * step, axis=0
+    )
+    for far in range(1, ways):
+        value = lax.ppermute(value, "seq", [(d, (d + 1) % ways) for d in range(ways)])
+        full = lax.dynamic_update_slice_in_dim(full, value, (here - far) % ways * step, axis=0)
+    piece_keys = full
     piece_values = lax.all_gather(values, "seq", axis=0, tiled=True)
     count = piece_keys.shape[0]
     length = block_length(count)

time: 291 us -> 263 us (0.904)
  waiting for transfers between devices: 188 us -> 120 us
  local copies, waits for them, and re-layouts: 38 us -> 64.8 us
  blocking collectives: 0 us -> 24.9 us
  starting transfers between devices: 11.6 us -> 3.1 us
    all_gather x1, waiting for transfers between devices: 31.1 us -> 0.01 us  [per_device(): piece_values = lax.all_gather(values, 'seq', axis=0, tiled=True)]
    all_gather x1, waiting for transfers between devices: 45.3 us -> 18.7 us  [per_device(): lax.all_gather(out_weight, 'dp', axis=0, tiled=True)]
    all_to_all x0 -> x1, blocking collectives: none -> 24.9 us  [per_device(): lax.all_to_all(pixels, 'dp', split_axis=0, concat_axis=0, tiled=True)]
    all_gather x1 -> x0, waiting for transfers between devices: 21.3 us -> none  [per_device(): piece_keys = lax.all_gather(key_rows, 'seq', axis=0, tiled=True)]
    ppermute x0 -> x7, waiting for transfers between devices: none -> 19.8 us  [per_device(): lax.ppermute(value, 'seq', [(d, (d + 1) % ways) for d in range(ways)])]
    ppermute x0 -> x7, local copies, waits for them, and re-layouts: none -> 13.1 us  [per_device(): lax.ppermute(value, 'seq', [(d, (d + 1) % ways) for d in range(ways)])]
    dynamic_update_slice x0 -> x8, local copies, waits for them, and re-layouts: none -> 13 us  [the longest x7 12.2 us: per_device(): lax.dynamic_update_slice_in_dim(full, value, (here - far) % ways * step,...]
    all_to_all x1 -> x0, starting transfers between devices: 11.4 us -> none  [per_device(): lax.all_to_all(pixels, 'dp', split_axis=0, concat_axis=0, tiled=True)]
  transfers between devices with their start and end apart: 5 -> 10, of which waited for: 5 -> 6; matrix products, arithmetic and copies ran while one was open for 17% -> 33% of each run, Pallas kernels for 0% -> 0%
where the time goes in v1:
time: 263 us; the launch traced here: 262 us
  waiting for transfers between devices  120 us (46%)
  local copies, waits for them, and re-layouts  64.8 us (25%)
  matrix products  25.6 us (10%)
  blocking collectives  24.9 us (9%)
  between operations  13.5 us (5%)
  other arithmetic  9.89 us (4%)
  starting transfers between devices  3.1 us (1%)
    all_gather x1, waiting for transfers between devices, per_device(): lax.all_gather(qkv_weight, 'dp', axis=0, tiled=True)  80.7 us
    all_to_all x1, blocking collectives, per_device(): lax.all_to_all(pixels, 'dp', split_axis=0, concat_axis=0, tiled=True)  24.9 us
    ppermute x7, waiting for transfers between devices, per_device(): lax.ppermute(value, 'seq', [(d, (d + 1) % ways) for d in range(ways)])  19.8 us
    all_gather x1, waiting for transfers between devices, per_device(): lax.all_gather(out_weight, 'dp', axis=0, tiled=True)  18.7 us
    ppermute x7, local copies, waits for them, and re-layouts, per_device(): lax.ppermute(value, 'seq', [(d, (d + 1) % ways) for d in range(ways)])  13.1 us
    dynamic_update_slice x7, local copies, waits for them, and re-layouts, per_device(): lax.dynamic_update_slice_in_dim(full, value, (here - far) % ways * step,...  12.2 us
    dot_general x2, matrix products, attend_block(): jnp.einsum('hqk,khd->qhd', weights.astype(jnp.bfloat16), value_block.resh...  9.94 us
    dynamic_slice x4, local copies, waits for them, and re-layouts, one_block(): value_block = lax.dynamic_slice_in_dim(piece_values, first_row, length, 0)  9.81 us
  transfers between devices with their start and end apart: 10, of which 6 were waited for; matrix products, arithmetic and copies ran while one was open for 33% of the time, Pallas kernels for 0%

profile of v1, /device:TPU:8, one launch (start us, length us, event | category | flops | bytes accessed | tf_op | source)
XLA Modules:
  0.0 261.8 jit_solution(9381264722090382059)
XLA Ops:
  6.5 0.7 all-gather.4.cloned.1.call-update
  7.3 2.0 copy.41
  9.3 1.1 all_to_all.8
  10.4 24.9 %all_to_all.12 = bf16[32,4,1176]{2,1,0:T(4,128)(2,1)} all-to-all(bf16[32,4,1176]{2,1,0:T(4,128)(2,1)S(1)} %all_to_all.8), channel_id=1, replica_groups=mesh['dp'=32,'seq'=8] {'dp'}, dimensions={0} | all-to-all | bytes 602112 | tf_op jit(solution)/shard_map/all_to_all | solution.py:97
  35.2 1.1 all_to_all.10
  36.4 0.7 fusion.28
  37.1 0.8 copy-done.2
  37.9 0.2 multiply_reduce_fusion
  38.2 80.7 %all-gather.4.cloned.1.call-done = bf16[1280,3840]{1,0:T(8,128)(2,1)} async-done(((bf16[40,3840]{1,0:T(8,128)(2,1)}), bf16[1280,3840]{1,0:T(8,128)(2,1)}) %all-gather.4.cloned.1.call-update) | async-done | bytes 9830416 | tf_op jit(solution)/shard_map/all_gather | solution.py:109
  118.9 5.5 %convolution_add_fusion = f32[128,3840]{1,0:T(8,128)S(1)} fusion(bf16[1280,3840]{1,0:T(8,128)(2,1)} %all-gather.4.cloned.1.call-done, f32[3840]{0:T(1024)S(1)} %copy-done.10, f32[128,1280]{1,0:T(8,128)} %copy-done.2, f32[1280]{0:T(1024)S(1)} %copy-done.7, f32[1280]{0:T(1024)S(1)} %copy-done.8, f32[128]{0:T(128)S(1)} %add_rsqrt_fusion, ...), kind=kOutput, calls=%fused_computation.24 | convolution fusion | flops 1259601920 | bytes 12478464 | tf_op jit(solution)/shard_map/dot_general | solution.py:107
  124.4 1.3 copy-done.3
  125.7 0.8 slice.41
  126.5 0.2 all-gather.8.cloned.1.call-start
  127.3 0.9 mul.220
  128.2 2.2 copy.42
  130.4 2.4 fusion.27
  132.9 2.2 copy.43
  135.0 2.2 copy.54
  137.2 1.4 slice_negate_fusion
  138.6 1.2 maximum_multiply_fusion.1
  139.8 2.2 copy.44
  142.0 2.2 copy.55
  144.2 2.8 %add_convert_fusion = (bf16[128,1280]{1,0:T(8,128)(2,1)}, bf16[128,1280]{1,0:T(8,128)(2,1)S(1)}) fusion(f32[128,1280]{1,0:T(8,128)} %copy.55, f32[128,1280]{1,0:T(8,128)} %copy.42, f32[128,3840]{1,0:T(8,128)} %copy-done.3, f32[128,1280]{1,0:T(8,128)} %copy.44), kind=kLoop, calls=%fused_computation.34 | loop fusion | flops 983040 | bytes 3932160 | tf_op jit(solution)/shard_map/convert_element_type | solution.py:121
  147.0 6.5 %collective-permute-done = bf16[128,1280]{1,0:T(8,128)(2,1)S(1)} collective-permute-done((bf16[128,1280]{1,0:T(8,128)(2,1)S(1)}, bf16[128,1280]{1,0:T(8,128)(2,1)S(1)}, u32[]{:S(2)}, u32[]{:S(2)}) %collective-permute-start) | collective-permute-done | bytes 327712 | tf_op jit(solution)/shard_map/ppermute | solution.py:147
  153.5 6.5 %collective-permute-done.1 = bf16[128,1280]{1,0:T(8,128)(2,1)S(1)} collective-permute-done((bf16[128,1280]{1,0:T(8,128)(2,1)S(1)}, bf16[128,1280]{1,0:T(8,128)(2,1)S(1)}, u32[]{:S(2)}, u32[]{:S(2)}) %collective-permute-start.1) | collective-permute-done | bytes 327712 | tf_op jit(solution)/shard_map/ppermute | solution.py:147
  160.0 0.7 copy-done.5
  160.7 6.6 %collective-permute-done.2 = bf16[128,1280]{1,0:T(8,128)(2,1)} collective-permute-done((bf16[128,1280]{1,0:T(8,128)(2,1)S(1)}, bf16[128,1280]{1,0:T(8,128)(2,1)}, u32[]{:S(2)}, u32[]{:S(2)}) %collective-permute-start.2) | collective-permute-done | bytes 327712 | tf_op jit(solution)/shard_map/ppermute | solution.py:147
  167.6 0.9 copy.45
  168.5 1.2 copy.56
  169.7 1.8 broadcast_in_dim.97
  171.5 0.8 constant_dynamic-update-slice_fusion.7
  172.3 1.9 copy.46
  174.2 1.6 collective-permute-start.4
  175.8 1.8 constant_dynamic-update-slice_fusion.6
  177.5 1.9 copy.47
  179.4 1.7 constant_dynamic-update-slice_fusion.5
  181.2 1.9 copy.48
  183.0 1.8 constant_dynamic-update-slice_fusion.4
  184.8 1.9 copy.49
  186.7 1.7 constant_dynamic-update-slice_fusion.3
  188.4 1.9 copy.50
  190.3 1.2 collective-permute-start.6
  191.5 1.7 constant_dynamic-update-slice_fusion.2
  193.2 1.9 copy.51
  195.1 1.8 constant_dynamic-update-slice_fusion.1
  196.9 0.2 collective-permute-done.6
  197.1 1.9 copy.52
  199.0 1.7 constant_dynamic-update-slice_fusion
  200.7 31.2 %while.20 = (s32[]{:T(128)}, f32[16,128]{1,0:T(8,128)S(1)}, f32[16,128]{1,0:T(8,128)S(1)}, f32[128,16,80]{0,2,1:T(8,128)}, s32[128]{0:T(128)S(1)}, /*index=5*/s3...) while((s32[]{:T(128)}, f32[16,128]{1,0:T(8,128)S(1)}, ...), condition=%wide.region_9.10_spmd.clone, body=%wide.region_5.9_spmd.clone.sunk | while | flops 349750272 | bytes 41890536 | solution.py:163
  200.7 1.4 constant_dynamic-slice_fusion.4
  202.4 3.0 %fusion.50 = (f32[16,128]{1,0:T(8,128)S(1)}, f32[16,512,128]{2,1,0:T(8,128)}) fusion(pred[128,512]{0,1:T(8,128)(4,1)S(1)} %broadcast_compare_fusion.2, bf16[512,16,80]{0,2,1:T(8,128)(2,1)S(1)} %bitcast.64, bf16[128,16,80]{0,2,1:T(8,128)(2,1)S(1)} %get-tuple-element.425), kind=kOutput, calls=%fused_computation.2.clone.1 | convolution fusion | flops 170915840 | bytes 5906432 | tf_op jit(solution)/shard_map/while/body/eval_jaxpr/qhd,khd->hqk/dot_general | solution.py:61
  205.4 2.5 constant_dynamic-slice_fusion.5
  207.8 2.4 copy.61
  210.3 4.8 %fusion.54 = f32[128,16,80]{0,2,1:T(8,128)} fusion(bf16[512,16,80]{0,2,1:T(8,128)(2,1)} %bitcast.65, f32[16,512,128]{2,1,0:T(8,128)} %get-tuple-element.390, f32[16,128]{1,0:T(8,128)S(1)} %get-tuple-element.419, pred[128,512]{0,1:T(8,128)(4,1)S(1)} %broadcast_compare_fusion.2, f32[128,16,80]{0,2,1:T(8,128)} %get-tuple-element.408, ...), kind=kOutput, calls=%fused_computation.8.clone.1 | convolution fusion | flops 173506560 | bytes 6897665 | tf_op jit(solution)/shard_map/while/body/eval_jaxpr/hqk,khd->qhd/dot_general | solution.py:75
  215.1 1.0 fusion.52
  216.2 1.4 constant_dynamic-slice_fusion.4
  217.9 3.0 %fusion.50 = (f32[16,128]{1,0:T(8,128)S(1)}, f32[16,512,128]{2,1,0:T(8,128)}) fusion(pred[128,512]{0,1:T(8,128)(4,1)S(1)} %broadcast_compare_fusion.2, bf16[512,16,80]{0,2,1:T(8,128)(2,1)S(1)} %bitcast.64, bf16[128,16,80]{0,2,1:T(8,128)(2,1)S(1)} %get-tuple-element.425), kind=kOutput, calls=%fused_computation.2.clone.1 | convolution fusion | flops 170915840 | bytes 5906432 | tf_op jit(solution)/shard_map/while/body/eval_jaxpr/qhd,khd->hqk/dot_general | solution.py:61
  220.9 2.5 constant_dynamic-slice_fusion.5
  223.3 2.4 copy.61
  225.8 5.1 %fusion.54 = f32[128,16,80]{0,2,1:T(8,128)} fusion(bf16[512,16,80]{0,2,1:T(8,128)(2,1)} %bitcast.65, f32[16,512,128]{2,1,0:T(8,128)} %get-tuple-element.390, f32[16,128]{1,0:T(8,128)S(1)} %get-tuple-element.419, pred[128,512]{0,1:T(8,128)(4,1)S(1)} %broadcast_compare_fusion.2, f32[128,16,80]{0,2,1:T(8,128)} %get-tuple-element.408, ...), kind=kOutput, calls=%fused_computation.8.clone.1 | convolution fusion | flops 173506560 | bytes 6897665 | tf_op jit(solution)/shard_map/while/body/eval_jaxpr/hqk,khd->qhd/dot_general | solution.py:75
  230.9 1.0 fusion.52
  231.9 1.1 divide_convert_fusion
  233.1 18.7 %all-gather.8.cloned.1.call-done = bf16[1280,1280]{1,0:T(8,128)(2,1)} async-done(((bf16[40,1280]{1,0:T(8,128)(2,1)}), bf16[1280,1280]{1,0:T(8,128)(2,1)}) %all-gather.8.cloned.1.call-update) | async-done | bytes 3276816 | tf_op jit(solution)/shard_map/all_gather | solution.py:172
  251.8 3.4 %fusion.18 = bf16[128,1280]{1,0:T(8,128)(2,1)} fusion(f32[128,1280]{1,0:T(8,128)} %copy-done.2, bf16[128,1280]{0,1:T(8,128)(2,1)S(1)} %bitcast.72, bf16[1280,1280]{1,0:T(8,128)(2,1)} %all-gather.8.cloned.1.call-done, f32[1280]{0:T(1024)S(1)} %copy-done.11), kind=kOutput, calls=%fused_computation.27 | convolution fusion | flops 419921920 | bytes 4592640 | tf_op jit(solution)/shard_map/dot_general | solution.py:170
  (66 shorter events, 1.3 us)
Async XLA Ops:
  6.5 29.8 %copy-start = (bf16[1176,1280]{1,0:T(8,128)(2,1)S(1)}, bf16[1176,1280]{1,0:T(8,128)(2,1)}, u32[]{:S(2)}) copy-start(bf16[1176,1280]{1,0:T(8,128)(2,1)} %param.13) | copy-start | bytes 9031684
  6.5 112.3 %all-gather.4.cloned.1.call-start = ((), (), s32[]{:S(2)}) async-start(), calls=%async_computation.1 | async-start | bytes 10137600 | tf_op jit(solution)/shard_map/all_gather | solution.py:109
  7.3 193.4 %all-gather.6.cloned.1.call-start = ((), (), s32[]{:S(2)}) async-start(), calls=%async_computation.2 | async-start | bytes 2949120 | tf_op jit(solution)/shard_map/all_gather | solution.py:150
  35.2 83.7 %copy-start.7 = (f32[1280]{0:T(1024)S(1)}, f32[1280]{0:T(1024)}, u32[]{:S(2)}) copy-start(f32[1280]{0:T(1024)} %param.15) | copy-start | bytes 15364
  35.2 83.7 %copy-start.8 = (f32[1280]{0:T(1024)S(1)}, f32[1280]{0:T(1024)}, u32[]{:S(2)}) copy-start(f32[1280]{0:T(1024)} %param.14) | copy-start | bytes 15364
  35.2 83.7 %copy-start.10 = (f32[3840]{0:T(1024)S(1)}, f32[3840]{0:T(1024)}, u32[]{:S(2)}) copy-start(f32[3840]{0:T(1024)} %param.17) | copy-start | bytes 46084
  37.1 0.9 copy-start.2
  38.1 88.6 %copy-start.9 = (s32[1,3]{1,0:T(1,128)S(1)}, s32[1,3]{1,0:T(1,128)}, u32[]{:S(2)}) copy-start(s32[1,3]{1,0:T(1,128)} %param.20) | copy-start | bytes 40
  38.2 88.7 %copy-start.12 = (s32[1,3]{1,0:T(1,128)S(1)}, s32[1,3]{1,0:T(1,128)}, u32[]{:S(2)}) copy-start(s32[1,3]{1,0:T(1,128)} %param.21) | copy-start | bytes 40
  124.4 1.3 copy-start.3
  126.5 125.3 %all-gather.8.cloned.1.call-start = ((), (), s32[]{:S(2)}) async-start(), calls=%async_computation.3 | async-start | bytes 3379200 | tf_op jit(solution)/shard_map/all_gather | solution.py:172
  147.0 6.5 %collective-permute-start = (bf16[128,1280]{1,0:T(8,128)(2,1)S(1)}, bf16[128,1280]{1,0:T(8,128)(2,1)S(1)}, u32[]{:S(2)}, u32[]{:S(2)}) collective-permute-start(bf16[128,1280]{1,0:T(8,128)(2,1)S(1)} %get-tuple-element.312), channel_id=1, source_target_pairs={{0,1},{1,2},{2,3},{3,4},{4,5},{5,6},{6,7},{7,0},{8,9},{9,10},{10,1... | collective-permute-start | bytes 983048 | tf_op jit(solution)/shard_map/ppermute | solution.py:147
  153.5 13.8 %copy-start.6 = (bf16[128,1280]{1,0:T(8,128)(2,1)}, bf16[128,1280]{1,0:T(8,128)(2,1)S(1)}, u32[]{:S(2)}) copy-start(bf16[128,1280]{1,0:T(8,128)(2,1)S(1)} %collective-permute-done) | copy-start | bytes 983044
  153.5 6.5 %collective-permute-start.1 = (bf16[128,1280]{1,0:T(8,128)(2,1)S(1)}, bf16[128,1280]{1,0:T(8,128)(2,1)S(1)}, u32[]{:S(2)}, u32[]{:S(2)}) collective-permute-start(bf16[128,1280]{1,0:T(8,128)(2,1)S(1)} %collective-permute-done), channel_id=1, source_target_pairs={{0,1},{1,2},{2,3},{3,4},{4,5},{5,6},{6,7},{7,0},{8,9},{9,10},{10,1... | collective-permute-start | bytes 983048 | tf_op jit(solution)/shard_map/ppermute | solution.py:147
  160.0 0.7 copy-start.5
  160.7 6.6 %collective-permute-start.2 = (bf16[128,1280]{1,0:T(8,128)(2,1)S(1)}, bf16[128,1280]{1,0:T(8,128)(2,1)}, u32[]{:S(2)}, u32[]{:S(2)}) collective-permute-start(bf16[128,1280]{1,0:T(8,128)(2,1)S(1)} %collective-permute-done.1), channel_id=1, source_target_pairs={{0,1},{1,2},{2,3},{3,4},{4,5},{5,6},{6,7},{7,0},{8,9},{9,10},{10,1... | collective-permute-start | bytes 983048 | tf_op jit(solution)/shard_map/ppermute | solution.py:147
  167.4 6.8 %collective-permute-start.3 = (bf16[128,1280]{1,0:T(8,128)(2,1)}, bf16[128,1280]{1,0:T(8,128)(2,1)}, u32[]{:S(2)}, u32[]{:S(2)}) collective-permute-start(bf16[128,1280]{1,0:T(8,128)(2,1)} %collective-permute-done.2), channel_id=1, source_target_pairs={{0,1},{1,2},{2,3},{3,4},{4,5},{5,6},{6,7},{7,0},{8,9},{9,10},{10,1... | collective-permute-start | bytes 983048 | tf_op jit(solution)/shard_map/ppermute | solution.py:147
  169.7 1.9 copy-start.4
  174.2 8.9 %collective-permute-start.4 = (bf16[128,1280]{1,0:T(8,128)(2,1)}, bf16[128,1280]{1,0:T(8,128)(2,1)}, u32[]{:S(2)}, u32[]{:S(2)}) collective-permute-start(bf16[128,1280]{1,0:T(8,128)(2,1)} %collective-permute-done.3), channel_id=1, source_target_pairs={{0,1},{1,2},{2,3},{3,4},{4,5},{5,6},{6,7},{7,0},{8,9},{9,10},{10,1... | collective-permute-start | bytes 983048 | tf_op jit(solution)/shard_map/ppermute | solution.py:147
  183.0 7.2 %collective-permute-start.5 = (bf16[128,1280]{1,0:T(8,128)(2,1)}, bf16[128,1280]{1,0:T(8,128)(2,1)}, u32[]{:S(2)}, u32[]{:S(2)}) collective-permute-start(bf16[128,1280]{1,0:T(8,128)(2,1)} %collective-permute-done.4), channel_id=1, source_target_pairs={{0,1},{1,2},{2,3},{3,4},{4,5},{5,6},{6,7},{7,0},{8,9},{9,10},{10,1... | collective-permute-start | bytes 983048 | tf_op jit(solution)/shard_map/ppermute | solution.py:147
  190.3 6.8 %collective-permute-start.6 = (bf16[128,1280]{1,0:T(8,128)(2,1)}, bf16[128,1280]{1,0:T(8,128)(2,1)}, u32[]{:S(2)}, u32[]{:S(2)}) collective-permute-start(bf16[128,1280]{1,0:T(8,128)(2,1)} %collective-permute-done.5), channel_id=1, source_target_pairs={{0,1},{1,2},{2,3},{3,4},{4,5},{5,6},{6,7},{7,0},{8,9},{9,10},{10,1... | collective-permute-start | bytes 983048 | tf_op jit(solution)/shard_map/ppermute | solution.py:147
  200.7 51.1 %copy-start.11 = (f32[1280]{0:T(1024)S(1)}, f32[1280]{0:T(1024)}, u32[]{:S(2)}) copy-start(f32[1280]{0:T(1024)} %param.19) | copy-start | bytes 15364
  210.3 4.9 %copy-start.1 = (f32[16,512,128]{2,1,0:T(8,128)S(1)}, f32[16,512,128]{2,1,0:T(8,128)}, u32[]{:S(2)}) copy-start(f32[16,512,128]{2,1,0:T(8,128)} %get-tuple-element.390) | copy-start | bytes 12582916 | tf_op jit(solution)/shard_map/while
  225.8 5.1 %copy-start.1 = (f32[16,512,128]{2,1,0:T(8,128)S(1)}, f32[16,512,128]{2,1,0:T(8,128)}, u32[]{:S(2)}) copy-start(f32[16,512,128]{2,1,0:T(8,128)} %get-tuple-element.390) | copy-start | bytes 12582916 | tf_op jit(solution)/shard_map/while
Sparse Core Ops, SparseCore 0:
  10.0 108.8 all-gather.3
  126.6 24.8 all-gather.5
  167.5 84.2 all-gather.7
